TPU v7x, 32 devices: a whole 2x2x4 slice. The times are simulated.
32 devices in a mesh: gx: 4 (over x, core), yz: 8 (over z, y).
Axes of the slice: x: 2, y: 2, z: 4, core: 2. Of those that a mesh axis runs over, the one named last changes fastest.
Arguments:
- hidden_in: bfloat16 [128, 12288], P('gx', 'yz'), may hold values from -2000 to 2000
- norm_gain: float32 [12288], P('yz'), may hold values from 0.1 to 1.9
- query_key_value_weight: bfloat16 [12288, 8, 1792], P('yz', 'gx'), may hold values from -0.0546875 to 0.0546875
- out_weight: bfloat16 [12288, 12288], P('gx', 'yz'), may hold values from -0.21875 to 0.21875
- key_cache: bfloat16 [128, 2048, 8, 128], P('yz', None, 'gx'), may hold values from -404 to 404
- cached_value_rows: bfloat16 [128, 2048, 8, 128], P('yz', None, 'gx'), may hold values from -6 to 6
- lengths: int32 [128], P('yz'), may hold values from 4 to 2048, as said below
Outputs:
- attn_out: bfloat16 [128, 12288], P('gx', 'yz')
Inputs may be any that keep to these rules, and one draw needn't show every extreme that they name: Row r's cache slots 0 to lengths[r] - 1 hold its tokens; the others are unused. Some row has 2048 cached tokens and some row has 4.
All inputs are finite; a program needn't handle non-finite values.
Results may differ from a plain program's by a relative error of at most 0.012.
The roundings to bfloat16 on the way count: a program that leaves them out, or rounds other values in their place, can miss the bound.
Values may be sent and summed in bfloat16 or wider, within the bound.
A program may use at most 192 MiB of HBM per device.

v0:
```python
import jax
import jax.numpy as jnp
from jax import lax
from jax.sharding import PartitionSpec as P

MODEL_WIDTH = 12288
HEAD_SIZE = 128
QUERIES_PER_KEY = 12


EPS = 1e-05
ROPE_BASE = 1000000.0


def rotate(block, positions):
    half_width = block.shape[-1] // 2
    frequency = ROPE_BASE ** (-(jnp.arange(half_width, dtype=jnp.float32) * 2.0) / block.shape[-1])
    angles = positions[..., None] * frequency
    cosine = jnp.cos(angles)
    sine = jnp.sin(angles)
    first = block[..., :half_width]
    second_part = block[..., half_width:]
    return jnp.concatenate(
        [first * cosine - second_part * sine, second_part * cosine + first * sine], axis=-1
    )


def body(
    hidden_in, norm_gain, query_key_value_weight, out_weight, key_cache, cached_value_rows, lengths
):
    inputs = hidden_in.astype(jnp.float32)
    squares = lax.psum(jnp.sum(inputs * inputs, axis=1), "yz")
    normed = (inputs * lax.rsqrt(squares[:, None] / MODEL_WIDTH + EPS) * norm_gain).astype(
        jnp.bfloat16
    )
    gathered = lax.all_gather(normed, "gx", axis=0, tiled=True)
    kv_local = query_key_value_weight.shape[1]
    weight_flat_matrix = query_key_value_weight.reshape(
        query_key_value_weight.shape[0], kv_local * query_key_value_weight.shape[2]
    )
    own_count = gathered.shape[0] // lax.axis_size("yz")
    block_rows = gathered
    projected_rows = lax.psum_scatter(
        jnp.dot(block_rows, weight_flat_matrix, preferred_element_type=jnp.float32),
        "yz",
        scatter_dimension=0,
        tiled=True,
    )
    projected_rows = projected_rows.reshape(own_count, kv_local, QUERIES_PER_KEY + 2, HEAD_SIZE)
    positions = lengths.astype(jnp.float32)
    queries = rotate(projected_rows[:, :, :QUERIES_PER_KEY], positions[:, None, None]).astype(
        jnp.bfloat16
    )
    new_keys = rotate(projected_rows[:, :, QUERIES_PER_KEY], positions[:, None]).astype(
        jnp.bfloat16
    )
    new_values = projected_rows[:, :, QUERIES_PER_KEY + 1].astype(jnp.bfloat16)
    factor = HEAD_SIZE ** (-0.5)
    valid = jnp.arange(key_cache.shape[1], dtype=jnp.int32)[None, :] < lengths[:, None]
    scores = (
        jnp.einsum("rkgd,rjkd->rkgj", queries, key_cache, preferred_element_type=jnp.float32)
        * factor
    )
    scores = jnp.where(valid[:, None, None, :], scores, -jnp.inf)
    own_score = (
        jnp.einsum("rkgd,rkd->rkg", queries, new_keys, preferred_element_type=jnp.float32) * factor
    )
    largest = jnp.maximum(jnp.max(scores, axis=-1), own_score)
    weights = jnp.exp(scores - largest[..., None])
    own_weight = jnp.exp(own_score - largest)
    totals = jnp.sum(weights, axis=-1) + own_weight
    probs = (weights / totals[..., None]).astype(jnp.bfloat16)
    own_prob = lax.optimization_barrier((own_weight / totals).astype(jnp.bfloat16)).astype(
        jnp.float32
    )
    mixed = jnp.einsum(
        "rkgj,rjkd->rkgd", probs, cached_value_rows, preferred_element_type=jnp.float32
    )
    mixed = mixed + own_prob[..., None] * new_values.astype(jnp.float32)[:, :, None, :]
    heads_out = mixed.astype(jnp.bfloat16).reshape(
        own_count, kv_local * QUERIES_PER_KEY * HEAD_SIZE
    )
    all_heads = lax.all_gather(heads_out, "yz", axis=0, tiled=True)
    block_rows = all_heads
    return lax.psum_scatter(
        jnp.dot(block_rows, out_weight, preferred_element_type=jnp.float32).astype(jnp.bfloat16),
        "gx",
        scatter_dimension=0,
        tiled=True,
    )


def solution(mesh):
    in_specs = (
        P("gx", "yz"),
        P("yz"),
        P("yz", "gx", None),
        P("gx", "yz"),
        P("yz", None, "gx", None),
        P("yz", None, "gx", None),
        P("yz"),
    )
    out_specs = P("gx", "yz")
    return jax.shard_map(body, mesh=mesh, in_specs=in_specs, out_specs=out_specs, check_vma=False)
```

profile of v0, /device:TPU:0, one launch (start us, length us, event | category | flops | bytes accessed | tf_op | source)
XLA Modules:
  0.0 209.1 jit_solution(6269504084988327509)
XLA Ops:
  6.5 0.0 reduce-scatter.3.cloned.1.call-start
  6.5 0.0 copy-start.1
  6.5 0.0 copy-start.2
  6.5 10.8 %copy.14 = bf16[192,8,2,1792]{3,1,2,0:T(8,128)(2,1)} copy(bf16[192,8,2,1792]{3,2,1,0:T(2,128)(2,1)} %bitcast.13) | data formatting | bytes 22020096
  17.4 0.0 copy-done.1
  17.4 0.1 fusion.17
  17.5 23.1 %psum.7 = f32[32]{0:T(128)S(1)} all-reduce(f32[32]{0:T(128)S(1)} %fusion.17), channel_id=1, replica_groups=mesh['gx'=4,'yz'=8] {'yz'}, use_global_device_ids=true, to_apply=%region_1.0 | all-reduce | flops 32 | bytes 256 | tf_op jit(solution)/shard_map/psum | solution.py:32
  40.6 0.0 copy-done.2
  40.6 0.1 fusion.19
  40.7 6.5 %all_gather.6 = bf16[128,1536]{1,0:T(8,128)(2,1)S(1)} all-gather(bf16[32,1536]{1,0:T(8,128)(2,1)S(1)} %fusion.19), channel_id=1, replica_groups=mesh['gx'=4,'yz'=8] {'gx'}, dimensions={0}, use_global_device_ids=true | all-gather | bytes 491520 | tf_op jit(solution)/shard_map/all_gather | solution.py:36
  47.2 0.0 copy-start.3
  47.2 7.0 %fusion.28 = f32[128,3584]{1,0:T(8,128)} fusion(bf16[128,1536]{1,0:T(8,128)(2,1)S(1)} %all_gather.6, bf16[1536,3584]{1,0:T(8,128)(2,1)} %bitcast.12), kind=kOutput, calls=%fused_computation.45 | convolution fusion | flops 1409286144 | bytes 13238272 | tf_op jit(solution)/shard_map/dot_general | solution.py:44
  54.2 0.0 reduce-scatter.3.cloned.1.call-update
  54.2 0.0 reduce-scatter.5.cloned.1.call-start
  54.3 0.0 copy-done.3
  54.3 0.1 multiply_cosine_fusion
  54.4 0.1 iota_compare_fusion
  54.5 62.9 %reduce-scatter.3.cloned.1.call-done = f32[16,3584]{1,0:T(8,128)} async-done(((f32[128,3584]{1,0:T(8,128)}), f32[16,3584]{1,0:T(8,128)}) %reduce-scatter.3.cloned.1.call-update) | async-done | bytes 229392 | tf_op jit(solution)/shard_map/reduce_scatter | solution.py:43
  117.4 1.0 reshape.157
  118.5 0.1 subtract_convert_fusion
  118.6 0.1 subtract_convert_fusion.1
  118.7 0.1 maximum_bitcast_fusion
  118.8 0.2 fusion.20
  119.1 12.2 %fusion.4 = (f32[16,2,12]{2,1,0:T(2,128)S(1)}, f32[16,2,12,2048]{3,2,1,0:T(8,128)}) fusion(pred[16,2048]{1,0:T(8,128)(4,1)S(1)} %iota_compare_fusion, bf16[16,2048,2,128]{3,2,1,0:T(2,128)(2,1)} %param.11, bf16[16,2,12,64]{3,2,1,0:T(8,128)(2,1)S(1)} %get-tuple-element.6, bf16[16,2,12,64]{3,2,1,0:T(8,128)(2,1)S(1)} %get-tuple-element.5), kind=kOutput, calls=%fused_computation.7 | convolution fusion | flops 203882112 | bytes 20055552 | tf_op jit(solution)/shard_map/rkgd,rjkd->rkgj/dot_general | solution.py:61
  131.3 0.0 copy-start
  131.3 3.6 %fusion.5 = f32[16,2,12]{2,1,0:T(2,128)S(1)} fusion(f32[16,2,12,2048]{3,2,1,0:T(8,128)} %get-tuple-element.14, f32[16,2,12]{2,1,0:T(2,128)S(1)} %multiply_maximum_fusion, pred[16,2048]{1,0:T(8,128)(4,1)S(1)} %iota_compare_fusion), kind=kLoop, calls=%fused_computation.8 | loop fusion | flops 3145344 | bytes 3181568 | tf_op jit(solution)/shard_map/reduce_sum | solution.py:71
  134.9 0.0 copy-done
  134.9 9.4 %fusion.14 = bf16[16,2,12,128]{3,2,1,0:T(8,128)(2,1)S(1)} fusion(bf16[16,2048,2,128]{3,2,1,0:T(2,128)(2,1)} %param.12, f32[16,2,12,2048]{3,2,1,0:T(8,128)S(1)} %copy-done, f32[16,2,12]{2,1,0:T(2,128)S(1)} %get-tuple-element.8, f32[16,2,12]{2,1,0:T(2,128)S(1)} %multiply_maximum_fusion, pred[16,2048]{1,0:T(8,128)(4,1)S(1)} %iota_compare_fusion, ...), kind=kOutput, calls=%fused_computation.16 | convolution fusion | flops 205406208 | bytes 20075008 | tf_op jit(solution)/shard_map/rkgj,rjkd->rkgd/dot_general | solution.py:76
  144.4 0.1 reshape.158
  144.5 32.0 %all_gather.7 = bf16[128,3072]{1,0:T(8,128)(2,1)S(1)} all-gather(bf16[16,3072]{1,0:T(8,128)(2,1)S(1)} %reshape.158), channel_id=1, replica_groups=mesh['gx'=4,'yz'=8] {'yz'}, dimensions={0}, use_global_device_ids=true | all-gather | bytes 884736 | tf_op jit(solution)/shard_map/all_gather | solution.py:83
  176.5 5.8 %convolution_convert_fusion = bf16[128,1536]{1,0:T(8,128)(2,1)} fusion(bf16[128,3072]{1,0:T(8,128)(2,1)S(1)} %all_gather.7, bf16[3072,1536]{1,0:T(8,128)(2,1)} %param.10), kind=kOutput, calls=%fused_computation.9 | convolution fusion | flops 1208156160 | bytes 10616832 | tf_op jit(solution)/shard_map/dot_general | solution.py:86
  182.4 0.0 reduce-scatter.5.cloned.1.call-update
  182.4 19.8 %reduce-scatter.5.cloned.1.call-done = bf16[32,1536]{1,0:T(8,128)(2,1)} async-done(((bf16[128,1536]{1,0:T(8,128)(2,1)}), bf16[32,1536]{1,0:T(8,128)(2,1)}) %reduce-scatter.5.cloned.1.call-update) | async-done | bytes 98320 | tf_op jit(solution)/shard_map/reduce_scatter | solution.py:85
  (8 shorter events, 0.1 us)
Async XLA Ops:
  6.5 110.9 %reduce-scatter.3.cloned.1.call-start = ((), (), s32[]{:S(2)}) async-start(), calls=%async_computation.2 | async-start | bytes 2064384 | tf_op jit(solution)/shard_map/reduce_scatter | solution.py:43
  6.5 10.8 %copy-start.1 = (bf16[32,1536]{1,0:T(8,128)(2,1)S(1)}, bf16[32,1536]{1,0:T(8,128)(2,1)}, u32[]{:S(2)}) copy-start(bf16[32,1536]{1,0:T(8,128)(2,1)} %param.7) | copy-start | bytes 294916
  6.5 34.1 %copy-start.2 = (f32[1536]{0:T(1024)S(1)}, f32[1536]{0:T(1024)}, u32[]{:S(2)}) copy-start(f32[1536]{0:T(1024)} %param.8) | copy-start | bytes 18436
  47.2 7.1 %copy-start.3 = (s32[16]{0:T(128)S(1)}, s32[16]{0:T(128)}, u32[]{:S(2)}) copy-start(s32[16]{0:T(128)} %param.13) | copy-start | bytes 196
  54.2 148.0 %reduce-scatter.5.cloned.1.call-start = ((), (), s32[]{:S(2)}) async-start(), calls=%async_computation.3 | async-start | bytes 491520 | tf_op jit(solution)/shard_map/reduce_scatter | solution.py:85
  131.3 3.6 %copy-start = (f32[16,2,12,2048]{3,2,1,0:T(8,128)S(1)}, f32[16,2,12,2048]{3,2,1,0:T(8,128)}, u32[]{:S(2)}) copy-start(f32[16,2,12,2048]{3,2,1,0:T(8,128)} %get-tuple-element.14) | copy-start | bytes 9437188
Sparse Core Ops, SparseCore 0:
  54.3 63.0 reduce-scatter.2
  182.5 19.6 reduce-scatter.4
where the time goes:
time: 209 us
  waiting for transfers between devices  82.8 us (40%)
  blocking collectives  61.6 us (29%)
  matrix products  34.7 us (17%)
  between operations  13.5 us (6%)
  local copies, waits for them, and re-layouts  12 us (6%)
  other arithmetic  4.41 us (2%)
    reduce_scatter x1, waiting for transfers between devices, body(): lax.psum_scatter(jnp.dot(block_rows, weight_flat_matrix, preferred_elemen...  62.9 us
    all_gather x1, blocking collectives, body(): all_heads = lax.all_gather(heads_out, 'yz', axis=0, tiled=True)  32 us
    psum x1, blocking collectives, body(): squares = lax.psum(jnp.sum(inputs * inputs, axis=1), 'yz')  23.1 us
    reduce_scatter x1, waiting for transfers between devices, body(): lax.psum_scatter(jnp.dot(block_rows, out_weight, preferred_element_type=j...  19.8 us
    dot_general x1, matrix products, body(): jnp.einsum('rkgd,rjkd->rkgj', queries, key_cache, preferred_element_type=...  12.2 us
    unnamed x9, local copies, waits for them, and re-layouts  10.8 us
    dot_general x1, matrix products, body(): jnp.einsum('rkgj,rjkd->rkgd', probs, cached_value_rows, preferred_element...  9.45 us
    dot_general x1, matrix products, body(): jnp.dot(block_rows, weight_flat_matrix, preferred_element_type=jnp.float32)  6.98 us
  transfers between devices with their start and end apart: 2, of which 2 were waited for; matrix products, arithmetic and copies ran while one was open for 0% of the time, Pallas kernels for 0%

commit v1 on v0

v1 whole, which is shorter than its diff:
```python
import functools

import jax
import jax.numpy as jnp
from jax import lax
from jax.experimental import pallas as pl
from jax.experimental.pallas import tpu as pltpu
from jax.sharding import PartitionSpec as P

HEAD_SIZE = 128
QUERIES_PER_KEY = 12
SLOTS = QUERIES_PER_KEY + 2

EPS = 1e-05
ROPE_BASE = 1000000.0
MESH = pl.DeviceIdType.MESH
VMEM = pl.BlockSpec(memory_space=pltpu.VMEM)
ANY = pl.BlockSpec(memory_space=pl.ANY)


def factors(n):
    inner = 1 << ((n.bit_length() - 1) // 2)
    return n // inner, inner


def greet(peers):
    barrier = pltpu.get_barrier_semaphore()
    for axis, index in peers:
        pl.semaphore_signal(barrier, inc=1, device_id={axis: index}, device_id_type=MESH)
    pl.semaphore_wait(barrier, len(peers))


def start_copy(src, dst, send_sem, recv_sem, axis, index):
    copy = pltpu.make_async_remote_copy(
        src_ref=src,
        dst_ref=dst,
        send_sem=send_sem,
        recv_sem=recv_sem,
        device_id={axis: index},
        device_id_type=MESH,
    )
    copy.start()
    return copy


def project_kernel(
    gx, yz, chunks,
    hidden_ref, gain_ref, weight_ref, out_ref,
    hid, squares, squares_in, normed, partial, inner_in, mid, outer_in,
    hid_send, hid_recv, sq_send, sq_recv, inner_send, inner_recv, outer_send, outer_recv,
):
    outer, inner = factors(yz)
    g = lax.axis_index("gx")
    i = lax.axis_index("yz")
    a = i // inner
    b = lax.rem(i, inner)
    greet(
        [("gx", lax.rem(g + d, gx)) for d in range(1, gx)]
        + [("yz", lax.rem(i + d, yz)) for d in range(1, yz)]
    )
    copies = []
    for d in range(1, gx):
        copies.append(
            start_copy(hidden_ref, hid.at[g], hid_send.at[d - 1], hid_recv.at[d - 1], "gx", lax.rem(g + d, gx))
        )
    hid[g] = hidden_ref[...]
    for copy in copies:
        copy.wait_recv()
    rows_each, depth = hidden_ref.shape
    rows = rows_each * gx
    x = hid[...].reshape(rows, depth).astype(jnp.float32)
    own = jnp.sum(x * x, axis=1, keepdims=True)
    squares[...] = jnp.broadcast_to(own, (rows, 128)).T[:8]
    sq_copies = []
    for d in range(1, yz):
        sq_copies.append(
            start_copy(squares, squares_in.at[d - 1], sq_send.at[d - 1], sq_recv.at[d - 1], "yz", lax.rem(i + d, yz))
        )
    total = squares[...]
    for d in range(1, yz):
        sq_copies[d - 1].wait_recv()
        total = total + squares_in[d - 1]
    column = jnp.broadcast_to(total[:1], (128, rows)).T[:, :1]
    scale = lax.rsqrt(column / (depth * yz) + EPS)
    normed[...] = (x * scale * gain_ref[...]).astype(jnp.bfloat16)
    copies += sq_copies

    kv = weight_ref.shape[0]
    per = chunks // kv
    width = weight_ref.shape[2] // per
    own_rows = rows // yz
    inner_copies, outer_copies = [], []

    def first(c):
        part = jnp.dot(
            normed[...],
            weight_ref[c // per, :, (c % per) * width : (c % per + 1) * width],
            preferred_element_type=jnp.float32,
        )
        for q in range(outer):
            for p in range(inner):
                start = (q * inner + p) * own_rows
                partial[c, p, q] = part[start : start + own_rows]
        here = []
        for d in range(1, inner):
            p = lax.rem(b + d, inner)
            here.append(
                start_copy(
                    partial.at[c, p], inner_in.at[c, d - 1], inner_send.at[c, d - 1], inner_recv.at[c, d - 1],
                    "yz", a * inner + p,
                )
            )
        inner_copies.append(here)

    def second(c):
        value = partial[c, b]
        for d in range(1, inner):
            inner_copies[c][d - 1].wait_recv()
            value = value + inner_in[c, d - 1]
        mid[c] = value
        here = []
        for d in range(1, outer):
            q = lax.rem(a + d, outer)
            here.append(
                start_copy(
                    mid.at[c, q], outer_in.at[c, d - 1], outer_send.at[c, d - 1], outer_recv.at[c, d - 1],
                    "yz", q * inner + b,
                )
            )
        outer_copies.append(here)

    for c in range(chunks):
        first(c)
        if c:
            second(c - 1)
    second(chunks - 1)
    for c in range(chunks):
        value = mid[c, a]
        for d in range(1, outer):
            outer_copies[c][d - 1].wait_recv()
            value = value + outer_in[c, d - 1]
        out_ref[:, c * width : (c + 1) * width] = value
    for copy in copies:
        copy.wait_send()
    for c in range(chunks):
        for copy in inner_copies[c] + outer_copies[c]:
            copy.wait_send()


def project(hidden, gain, weight, gx, yz):
    outer, inner = factors(yz)
    rows_each, depth = hidden.shape
    rows = rows_each * gx
    kv, _, columns = weight.shape
    per = 2
    chunks = kv * per
    width = columns // per
    own = rows // yz
    dma = pltpu.SemaphoreType.DMA
    return pl.pallas_call(
        functools.partial(project_kernel, gx, yz, chunks),
        out_shape=jax.ShapeDtypeStruct((own, kv * columns), jnp.float32),
        in_specs=[VMEM, VMEM, VMEM],
        out_specs=VMEM,
        scratch_shapes=[
            pltpu.VMEM((gx, rows_each, depth), jnp.bfloat16),
            pltpu.VMEM((8, rows), jnp.float32),
            pltpu.VMEM((yz - 1, 8, rows), jnp.float32),
            pltpu.VMEM((rows, depth), jnp.bfloat16),
            pltpu.VMEM((chunks, inner, outer, own, width), jnp.float32),
            pltpu.VMEM((chunks, inner - 1, outer, own, width), jnp.float32),
            pltpu.VMEM((chunks, outer, own, width), jnp.float32),
            pltpu.VMEM((chunks, outer - 1, own, width), jnp.float32),
            dma((gx - 1,)), dma((gx - 1,)),
            dma((yz - 1,)), dma((yz - 1,)),
            dma((chunks, inner - 1)), dma((chunks, inner - 1)),
            dma((chunks, outer - 1)), dma((chunks, outer - 1)),
        ],
        compiler_params=pltpu.CompilerParams(
            collective_id=0, has_side_effects=True, vmem_limit_bytes=40 * 2**20
        ),
        name="project",
    )(hidden, gain, weight)


CHUNK = 512


def attend_kernel(
    kv, lengths_ref, proj_ref, cos_ref, sin_ref, key_ref, value_ref, out_ref,
    keys, values, queries, new_keys, new_values, scores, mixed, key_sem, value_sem,
):
    rows = proj_ref.shape[0]
    heads = kv * QUERIES_PER_KEY
    span = CHUNK * kv

    def count(r):
        return (lengths_ref[r] + CHUNK - 1) // CHUNK

    def copy_of(source, target, sems, r, c):
        part = pl.ds(pl.multiple_of(c * span, span), span)
        return pltpu.make_async_copy(source.at[r, part], target.at[r, part], sems.at[r, c])

    def begin(r, _):
        def each(c, _):
            copy_of(key_ref, keys, key_sem, r, c).start()
            copy_of(value_ref, values, value_sem, r, c).start()
            return 0

        return lax.fori_loop(0, count(r), each, 0)

    lax.fori_loop(0, rows, begin, 0)

    cosine, sine = cos_ref[...], sin_ref[...]
    for k in range(kv):
        for s in range(SLOTS):
            at = (k * SLOTS + s) * HEAD_SIZE
            x = proj_ref[:, at : at + HEAD_SIZE]
            if s <= QUERIES_PER_KEY:
                x = x * cosine + pltpu.roll(x, HEAD_SIZE // 2, 1) * sine
            x = x.astype(jnp.bfloat16).astype(jnp.float32)
            if s < QUERIES_PER_KEY:
                queries[:, k * QUERIES_PER_KEY + s, :] = x
            else:
                target = new_keys if s == QUERIES_PER_KEY else new_values
                for h in range(QUERIES_PER_KEY):
                    target[:, k * QUERIES_PER_KEY + h, :] = x

    factor = HEAD_SIZE ** (-0.5)
    column = lax.broadcasted_iota(jnp.int32, (heads, span), 1)
    head = lax.broadcasted_iota(jnp.int32, (heads, span), 0) // QUERIES_PER_KEY
    slot = column // kv
    slot = jnp.where(column - slot * kv == head, slot, 2**30)

    def row(r, _):
        length = lengths_ref[r]
        n = count(r)
        q32 = queries[r]
        q = q32.astype(jnp.bfloat16)
        own = jnp.sum(q32 * new_keys[r], axis=1, keepdims=True) * factor

        def score(c, largest):
            copy_of(key_ref, keys, key_sem, r, c).wait()
            part = pl.ds(pl.multiple_of(c * span, span), span)
            s = lax.dot_general(
                q, keys[r, part, :], (((1,), (1,)), ((), ())), preferred_element_type=jnp.float32
            ) * factor
            s = jnp.where(slot < length - c * CHUNK, s, -jnp.inf)
            scores[c] = s
            return jnp.maximum(largest, jnp.max(s, axis=1, keepdims=True))

        largest = lax.fori_loop(0, n, score, own)

        def weigh(c, total):
            w = jnp.exp(scores[c] - largest)
            scores[c] = w
            return total + jnp.sum(w, axis=1, keepdims=True)

        own_weight = jnp.exp(own - largest)
        total = lax.fori_loop(0, n, weigh, jnp.zeros((heads, 1), jnp.float32)) + own_weight

        def mix(c, acc):
            copy_of(value_ref, values, value_sem, r, c).wait()
            part = pl.ds(pl.multiple_of(c * span, span), span)
            probs = (scores[c] / total).astype(jnp.bfloat16)
            return acc + jnp.dot(probs, values[r, part, :], preferred_element_type=jnp.float32)

        acc = lax.fori_loop(0, n, mix, jnp.zeros((heads, HEAD_SIZE), jnp.float32))
        own_prob = (own_weight / total).astype(jnp.bfloat16).astype(jnp.float32)
        mixed[r] = acc + own_prob * new_values[r]
        return 0

    lax.fori_loop(0, rows, row, 0)
    for h in range(heads):
        out_ref[:, h * HEAD_SIZE : (h + 1) * HEAD_SIZE] = mixed[:, h, :].astype(jnp.bfloat16)


def attend(lengths, proj, cosine, sine, keys, values, kv):
    rows, flat, _ = keys.shape
    heads = kv * QUERIES_PER_KEY
    chunks = flat // kv // CHUNK
    return pl.pallas_call(
        functools.partial(attend_kernel, kv),
        out_shape=jax.ShapeDtypeStruct((rows, heads * HEAD_SIZE), jnp.bfloat16),
        in_specs=[pl.BlockSpec(memory_space=pltpu.SMEM), VMEM, VMEM, VMEM, ANY, ANY],
        out_specs=VMEM,
        scratch_shapes=[
            pltpu.VMEM((rows, flat, HEAD_SIZE), jnp.bfloat16),
            pltpu.VMEM((rows, flat, HEAD_SIZE), jnp.bfloat16),
            pltpu.VMEM((rows, heads, HEAD_SIZE), jnp.float32),
            pltpu.VMEM((rows, heads, HEAD_SIZE), jnp.float32),
            pltpu.VMEM((rows, heads, HEAD_SIZE), jnp.float32),
            pltpu.VMEM((chunks, heads, CHUNK * kv), jnp.float32),
            pltpu.VMEM((rows, heads, HEAD_SIZE), jnp.float32),
            pltpu.SemaphoreType.DMA((rows, chunks)),
            pltpu.SemaphoreType.DMA((rows, chunks)),
        ],
        compiler_params=pltpu.CompilerParams(vmem_limit_bytes=44 * 2**20),
        name="attend",
    )(lengths, proj, cosine, sine, keys, values)


def output_kernel(
    gx, yz, chunks, heads_ref, weight_ref, out_ref,
    gathered, partial, partial_in,
    outer_send, outer_recv, inner_send, inner_recv, sum_send, sum_recv,
):
    outer, inner = factors(yz)
    g = lax.axis_index("gx")
    i = lax.axis_index("yz")
    a = i // inner
    b = lax.rem(i, inner)
    own_rows, depth = heads_ref.shape
    rows = own_rows * yz
    greet(
        [("gx", lax.rem(g + d, gx)) for d in range(1, gx)]
        + [("yz", lax.rem(a + d, outer) * inner + b) for d in range(1, outer)]
        + [("yz", a * inner + lax.rem(b + d, inner)) for d in range(1, inner)]
    )
    outer_copies, inner_copies = [], []
    for d in range(1, outer):
        outer_copies.append(
            start_copy(
                heads_ref, gathered.at[a, b], outer_send.at[d - 1], outer_recv.at[d - 1],
                "yz", lax.rem(a + d, outer) * inner + b,
            )
        )

    def relay(source, q, e):
        for d in range(1, inner):
            inner_copies.append(
                start_copy(
                    source, gathered.at[q, b], inner_send.at[e, d - 1], inner_recv.at[e, d - 1],
                    "yz", a * inner + lax.rem(b + d, inner),
                )
            )

    relay(heads_ref, a, 0)
    gathered[a, b] = heads_ref[...]
    for d in range(1, outer):
        outer_copies[d - 1].wait_recv()
        q = lax.rem(a + outer - d, outer)
        relay(gathered.at[q, b], q, d)
    for copy in inner_copies:
        copy.wait_recv()

    width = out_ref.shape[1] // chunks
    rows_each = rows // gx
    sums = []
    for c in range(chunks):
        part = jnp.dot(
            gathered[...].reshape(rows, depth),
            weight_ref[:, c * width : (c + 1) * width],
            preferred_element_type=jnp.float32,
        ).astype(jnp.bfloat16)
        for p in range(gx):
            partial[c, p] = part[p * rows_each : (p + 1) * rows_each]
        here = []
        for d in range(1, gx):
            p = lax.rem(g + d, gx)
            here.append(
                start_copy(
                    partial.at[c, p], partial_in.at[c, d - 1], sum_send.at[c, d - 1], sum_recv.at[c, d - 1], "gx", p
                )
            )
        sums.append(here)
    for c in range(chunks):
        value = partial[c, g].astype(jnp.float32)
        for d in range(1, gx):
            sums[c][d - 1].wait_recv()
            value = value + partial_in[c, d - 1].astype(jnp.float32)
        out_ref[:, c * width : (c + 1) * width] = value.astype(jnp.bfloat16)
    for copy in outer_copies + inner_copies:
        copy.wait_send()
    for here in sums:
        for copy in here:
            copy.wait_send()


def output(heads, weight, gx, yz):
    outer, inner = factors(yz)
    own, depth = heads.shape
    rows = own * yz
    columns = weight.shape[1]
    chunks = 3
    width = columns // chunks
    dma = pltpu.SemaphoreType.DMA
    return pl.pallas_call(
        functools.partial(output_kernel, gx, yz, chunks),
        out_shape=jax.ShapeDtypeStruct((rows // gx, columns), jnp.bfloat16),
        in_specs=[VMEM, VMEM],
        out_specs=VMEM,
        scratch_shapes=[
            pltpu.VMEM((outer, inner, own, depth), jnp.bfloat16),
            pltpu.VMEM((chunks, gx, rows // gx, width), jnp.bfloat16),
            pltpu.VMEM((chunks, gx - 1, rows // gx, width), jnp.bfloat16),
            dma((outer - 1,)), dma((outer - 1,)),
            dma((outer, inner - 1)), dma((outer, inner - 1)),
            dma((chunks, gx - 1)), dma((chunks, gx - 1)),
        ],
        compiler_params=pltpu.CompilerParams(
            collective_id=1, has_side_effects=True, vmem_limit_bytes=24 * 2**20
        ),
        name="output",
    )(heads, weight)


def body(
    hidden_in, norm_gain, query_key_value_weight, out_weight, key_cache, cached_value_rows, lengths
):
    gx, yz = lax.axis_size("gx"), lax.axis_size("yz")
    own, cached, kv, size = key_cache.shape
    proj = project(
        hidden_in, norm_gain.reshape(1, -1), jnp.transpose(query_key_value_weight, (1, 0, 2)), gx, yz
    )
    half = size // 2
    frequency = ROPE_BASE ** (-(jnp.arange(half, dtype=jnp.float32) * 2.0) / size)
    angles = lengths.astype(jnp.float32)[:, None] * frequency
    cosine, sine = jnp.cos(angles), jnp.sin(angles)
    heads = attend(
        lengths,
        proj,
        jnp.concatenate([cosine, cosine], axis=1),
        jnp.concatenate([-sine, sine], axis=1),
        key_cache.reshape(own, cached * kv, size),
        cached_value_rows.reshape(own, cached * kv, size),
        kv,
    )
    return output(heads, out_weight, gx, yz)


def solution(mesh):
    in_specs = (
        P("gx", "yz"),
        P("yz"),
        P("yz", "gx", None),
        P("gx", "yz"),
        P("yz", None, "gx", None),
        P("yz", None, "gx", None),
        P("yz"),
    )
    out_specs = P("gx", "yz")
    return jax.shard_map(body, mesh=mesh, in_specs=in_specs, out_specs=out_specs, check_vma=False)
```

time: 209 us -> 102 us (0.49)
  Pallas kernels: 0 us -> 91.5 us
  waiting for transfers between devices: 82.8 us -> 0 us
  blocking collectives: 61.6 us -> 0 us
  matrix products: 34.7 us -> 0 us
  between operations: 13.5 us -> 0.11 us
  other arithmetic: 4.41 us -> 0.21 us
  local copies, waits for them, and re-layouts: 12 us -> 8.57 us
    pallas_call x0 -> x3, Pallas kernels: none -> 91.5 us  [the longest x1 44.5 us: project(): pl.pallas_call(functools.partial(project_kernel, gx, yz, chunks), out_sha...]
    reduce_scatter x2 -> x0, waiting for transfers between devices: 82.8 us -> none  [the longest x1 62.9 us: body(): lax.psum_scatter(jnp.dot(block_rows, weight_flat_matrix, preferred_elemen...]
    all_gather x2 -> x0, blocking collectives: 38.5 us -> none  [the longest x1 32 us: body(): all_heads = lax.all_gather(heads_out, 'yz', axis=0, tiled=True)]
    dot_general x5 -> x0, matrix products: 34.7 us -> none  [the longest x1 12.2 us: body(): jnp.einsum('rkgd,rjkd->rkgj', queries, key_cache, preferred_element_type=...]
    psum x1 -> x0, blocking collectives: 23.1 us -> none  [body(): squares = lax.psum(jnp.sum(inputs * inputs, axis=1), 'yz')]
    reduce_sum x2 -> x0, other arithmetic: 3.69 us -> none  [the longest x1 3.56 us: body(): totals = jnp.sum(weights, axis=-1) + own_weight]
    unnamed x9 -> x12, local copies, waits for them, and re-layouts: 10.8 us -> 7.87 us
  transfers between devices with their start and end apart: 2 -> 0, of which waited for: 2 -> 0; matrix products, arithmetic and copies ran while one was open for 0% -> 0% of each run, Pallas kernels for 0% -> 0%
where the time goes in v1:
time: 102 us; the launch traced here: 100 us
  Pallas kernels  91.5 us (90%)
  local copies, waits for them, and re-layouts  8.57 us (8%)
    pallas_call x1, Pallas kernels, project(): pl.pallas_call(functools.partial(project_kernel, gx, yz, chunks), out_sha...  44.5 us
    pallas_call x1, Pallas kernels, attend(): pl.pallas_call(functools.partial(attend_kernel, kv), out_shape=jax.ShapeD...  25.6 us
    pallas_call x1, Pallas kernels, output(): pl.pallas_call(functools.partial(output_kernel, gx, yz, chunks), out_shap...  21.5 us
    unnamed x12, local copies, waits for them, and re-layouts  7.87 us

profile of v1, /device:TPU:0, one launch (start us, length us, event | category | flops | bytes accessed | tf_op | source)
XLA Modules:
  0.0 100.4 jit_solution(15591501052514094720)
XLA Ops:
  0.0 0.7 reshape.17.gain_ref
  0.7 0.0 copy-start
  0.7 7.2 %copy.10 = bf16[1536,2,1792]{2,0,1:T(8,128)(2,1)S(1)} copy(bf16[1536,2,1792]{2,1,0:T(2,128)(2,1)} %param.9) | data formatting | bytes 22020096 | tf_op args[2]
  7.9 0.0 copy-start.1
  7.9 0.0 copy-done
  7.9 0.0 slice-start
  7.9 44.5 %project.1.proj_ref = f32[16,3584]{1,0:T(8,128)S(1)} custom-call(bf16[32,1536]{1,0:T(8,128)(2,1)S(1)} %copy-done, f32[1,1536]{1,0:T(1,128)S(1)} %reshape.17.gain_ref, bf16[2,1536,1792]{2,1,0:T(8,128)(2,1)S(1)} %bitcast.5), custom_call_target="tpu_custom_call" | custom-call | tf_op jit(solution)/shard_map/project/pallas_call | solution.py:160
  52.4 0.0 copy-done.1
  52.5 0.1 fusion
  52.6 0.1 pad_maximum_fusion
  52.7 0.0 slice-start.1
  52.7 0.0 slice-start.2
  52.7 25.6 %attend.1.heads_ref = bf16[16,3072]{1,0:T(8,128)(2,1)S(1)} custom-call(s32[16]{0:T(128)S(1)} %copy-done.1, f32[16,3584]{1,0:T(8,128)S(1)} %project.1.proj_ref, f32[16,128]{1,0:T(8,128)S(1)} %get-tuple-element.8.cos_ref, f32[16,128]{1,0:T(8,128)S(1)} %get-tuple-element.9.sin_ref, bf16[16,4096,128]{2,1,0:T(8,128)(2,1)} %bitcast.8, bf16[16,4096,128]{2,1,0:T(8,128)(2,1)} %bitcast.9), custom_call_target="tpu_custom_call" | custom-call | tf_op jit(solution)/shard_map/attend/pallas_call | solution.py:282
  78.2 0.0 slice-done
  78.2 0.0 slice-done.1
  78.3 0.0 slice-done.2
  78.3 21.5 %output.1 = bf16[32,1536]{1,0:T(8,128)(2,1)S(1)} custom-call(bf16[16,3072]{1,0:T(8,128)(2,1)S(1)} %attend.1.heads_ref, bf16[3072,1536]{1,0:T(8,128)(2,1)S(1)} %bitcast.7), custom_call_target="tpu_custom_call" | custom-call | tf_op jit(solution)/shard_map/output/pallas_call | solution.py:388
  99.8 0.6 copy.12
  (3 shorter events, 0.0 us)
Async XLA Ops:
  0.7 7.2 %copy-start = (bf16[32,1536]{1,0:T(8,128)(2,1)S(1)}, bf16[32,1536]{1,0:T(8,128)(2,1)}, u32[]{:S(2)}) copy-start(bf16[32,1536]{1,0:T(8,128)(2,1)} %hidden_ref.1) | copy-start | bytes 294916
  7.9 44.5 %copy-start.1 = (s32[16]{0:T(128)S(1)}, s32[16]{0:T(128)}, u32[]{:S(2)}) copy-start(s32[16]{0:T(128)} %lengths_ref.1) | copy-start | bytes 196
  7.9 70.3 %slice-start = ((s8[9437184]{0:T(1024)(128)(4,1)}), s8[1048576]{0:T(1024)(128)(4,1)S(1)}, s32[]{:S(2)}) async-start(s8[9437184]{0:T(1024)(128)(4,1)} %bitcast.6), calls=%async_computation | async-start | bytes 2097152
  52.7 25.6 %slice-start.1 = ((s8[9437184]{0:T(1024)(128)(4,1)}), s8[4194304]{0:T(1024)(128)(4,1)S(1)}, s32[]{:S(2)}) async-start(s8[9437184]{0:T(1024)(128)(4,1)} %bitcast.6), calls=%async_computation.1 | async-start | bytes 8388608
  52.7 25.6 %slice-start.2 = ((s8[9437184]{0:T(1024)(128)(4,1)}), s8[4194304]{0:T(1024)(128)(4,1)S(1)}, s32[]{:S(2)}) async-start(s8[9437184]{0:T(1024)(128)(4,1)} %bitcast.6), calls=%async_computation.2 | async-start | bytes 8388608

commit v2 on v1

--- a/solution.py
+++ b/solution.py
@@ -152,7 +152,7 @@
     rows_each, depth = hidden.shape
     rows = rows_each * gx
     kv, _, columns = weight.shape
-    per = 2
+    per = columns // 256
     chunks = kv * per
     width = columns // per
     own = rows // yz
@@ -177,7 +177,7 @@
             dma((chunks, outer - 1)), dma((chunks, outer - 1)),
         ],
         compiler_params=pltpu.CompilerParams(
-            collective_id=0, has_side_effects=True, vmem_limit_bytes=40 * 2**20
+            collective_id=0, has_side_effects=True, vmem_limit_bytes=10 * 2**20
         ),
         name="project",
     )(hidden, gain, weight)
@@ -188,23 +188,24 @@
 
 def attend_kernel(
     kv, lengths_ref, proj_ref, cos_ref, sin_ref, key_ref, value_ref, out_ref,
-    keys, values, queries, new_keys, new_values, scores, mixed, key_sem, value_sem,
+    values, queries, new_keys, new_values, scores, mixed, value_sem,
 ):
     rows = proj_ref.shape[0]
     heads = kv * QUERIES_PER_KEY
     span = CHUNK * kv
 
     def count(r):
-        return (lengths_ref[r] + CHUNK - 1) // CHUNK
-
-    def copy_of(source, target, sems, r, c):
+        first = r // 2 * 2
+        longer = jnp.maximum(lengths_ref[first], lengths_ref[first + 1])
+        return (longer + CHUNK - 1) // CHUNK
+
+    def copy_of(r, c):
         part = pl.ds(pl.multiple_of(c * span, span), span)
-        return pltpu.make_async_copy(source.at[r, part], target.at[r, part], sems.at[r, c])
+        return pltpu.make_async_copy(value_ref.at[r, part], values.at[r, part], value_sem.at[r, c])
 
     def begin(r, _):
         def each(c, _):
-            copy_of(key_ref, keys, key_sem, r, c).start()
-            copy_of(value_ref, values, value_sem, r, c).start()
+            copy_of(r, c).start()
             return 0
 
         return lax.fori_loop(0, count(r), each, 0)
@@ -232,45 +233,64 @@
     slot = column // kv
     slot = jnp.where(column - slot * kv == head, slot, 2**30)
 
-    def row(r, _):
-        length = lengths_ref[r]
-        n = count(r)
-        q32 = queries[r]
-        q = q32.astype(jnp.bfloat16)
-        own = jnp.sum(q32 * new_keys[r], axis=1, keepdims=True) * factor
-
-        def score(c, largest):
-            copy_of(key_ref, keys, key_sem, r, c).wait()
-            part = pl.ds(pl.multiple_of(c * span, span), span)
-            s = lax.dot_general(
-                q, keys[r, part, :], (((1,), (1,)), ((), ())), preferred_element_type=jnp.float32
-            ) * factor
-            s = jnp.where(slot < length - c * CHUNK, s, -jnp.inf)
-            scores[c] = s
-            return jnp.maximum(largest, jnp.max(s, axis=1, keepdims=True))
-
-        largest = lax.fori_loop(0, n, score, own)
-
-        def weigh(c, total):
-            w = jnp.exp(scores[c] - largest)
-            scores[c] = w
-            return total + jnp.sum(w, axis=1, keepdims=True)
-
-        own_weight = jnp.exp(own - largest)
-        total = lax.fori_loop(0, n, weigh, jnp.zeros((heads, 1), jnp.float32)) + own_weight
-
-        def mix(c, acc):
-            copy_of(value_ref, values, value_sem, r, c).wait()
-            part = pl.ds(pl.multiple_of(c * span, span), span)
-            probs = (scores[c] / total).astype(jnp.bfloat16)
-            return acc + jnp.dot(probs, values[r, part, :], preferred_element_type=jnp.float32)
-
-        acc = lax.fori_loop(0, n, mix, jnp.zeros((heads, HEAD_SIZE), jnp.float32))
-        own_prob = (own_weight / total).astype(jnp.bfloat16).astype(jnp.float32)
-        mixed[r] = acc + own_prob * new_values[r]
+    def pair(r, n):
+        both = (0, 1)
+        q32 = [queries[r + e] for e in both]
+        lengths = [lengths_ref[r + e] for e in both]
+        own = [jnp.sum(q32[e] * new_keys[r + e], axis=1, keepdims=True) * factor for e in both]
+        largest = [None, None]
+        for c in range(n):
+            for e in both:
+                s = lax.dot_general(
+                    q32[e].astype(jnp.bfloat16),
+                    key_ref[r + e, c * span : (c + 1) * span, :],
+                    (((1,), (1,)), ((), ())),
+                    preferred_element_type=jnp.float32,
+                ) * factor
+                s = jnp.where(slot < lengths[e] - c * CHUNK, s, -jnp.inf)
+                scores[e, c] = s
+                best = functools.reduce(
+                    jnp.maximum, [s[:, t : t + 128] for t in range(0, span, 128)]
+                )
+                largest[e] = best if c == 0 else jnp.maximum(largest[e], best)
+        largest = [
+            jnp.maximum(jnp.max(largest[e], axis=1, keepdims=True), own[e]) for e in both
+        ]
+        own_weight = [jnp.exp(own[e] - largest[e]) for e in both]
+        total = [None, None]
+        for c in range(n):
+            for e in both:
+                w = jnp.exp(scores[e, c] - largest[e])
+                scores[e, c] = w
+                add = functools.reduce(
+                    lambda x, y: x + y, [w[:, t : t + 128] for t in range(0, span, 128)]
+                )
+                total[e] = add if c == 0 else total[e] + add
+        total = [jnp.sum(total[e], axis=1, keepdims=True) + own_weight[e] for e in both]
+        inverse = [1.0 / total[e] for e in both]
+        for c in range(n):
+            for e in both:
+                copy_of(r + e, c).wait()
+        for e in both:
+            acc = jnp.zeros((heads, HEAD_SIZE), jnp.float32)
+            for c in range(n):
+                probs = (scores[e, c] * inverse[e]).astype(jnp.bfloat16)
+                acc = acc + jnp.dot(
+                    probs,
+                    values[r + e, c * span : (c + 1) * span, :],
+                    preferred_element_type=jnp.float32,
+                )
+            own_prob = (own_weight[e] * inverse[e]).astype(jnp.bfloat16).astype(jnp.float32)
+            mixed[r + e] = acc + own_prob * new_values[r + e]
+
+    def step(p, _):
+        r = p * 2
+        needed = count(r)
+        for n in range(1, scores.shape[1] + 1):
+            pl.when(needed == n)(functools.partial(pair, r, n))
         return 0
 
-    lax.fori_loop(0, rows, row, 0)
+    lax.fori_loop(0, rows // 2, step, 0)
     for h in range(heads):
         out_ref[:, h * HEAD_SIZE : (h + 1) * HEAD_SIZE] = mixed[:, h, :].astype(jnp.bfloat16)
 
@@ -282,20 +302,18 @@
     return pl.pallas_call(
         functools.partial(attend_kernel, kv),
         out_shape=jax.ShapeDtypeStruct((rows, heads * HEAD_SIZE), jnp.bfloat16),
-        in_specs=[pl.BlockSpec(memory_space=pltpu.SMEM), VMEM, VMEM, VMEM, ANY, ANY],
+        in_specs=[pl.BlockSpec(memory_space=pltpu.SMEM), VMEM, VMEM, VMEM, VMEM, ANY],
         out_specs=VMEM,
         scratch_shapes=[
-            pltpu.VMEM((rows, flat, HEAD_SIZE), jnp.bfloat16),
             pltpu.VMEM((rows, flat, HEAD_SIZE), jnp.bfloat16),
             pltpu.VMEM((rows, heads, HEAD_SIZE), jnp.float32),
             pltpu.VMEM((rows, heads, HEAD_SIZE), jnp.float32),
             pltpu.VMEM((rows, heads, HEAD_SIZE), jnp.float32),
-            pltpu.VMEM((chunks, heads, CHUNK * kv), jnp.float32),
+            pltpu.VMEM((2, chunks, heads, CHUNK * kv), jnp.float32),
             pltpu.VMEM((rows, heads, HEAD_SIZE), jnp.float32),
             pltpu.SemaphoreType.DMA((rows, chunks)),
-            pltpu.SemaphoreType.DMA((rows, chunks)),
         ],
-        compiler_params=pltpu.CompilerParams(vmem_limit_bytes=44 * 2**20),
+        compiler_params=pltpu.CompilerParams(vmem_limit_bytes=22 * 2**20),
         name="attend",
     )(lengths, proj, cosine, sine, keys, values)
 
@@ -399,7 +417,7 @@
             dma((chunks, gx - 1)), dma((chunks, gx - 1)),
         ],
         compiler_params=pltpu.CompilerParams(
-            collective_id=1, has_side_effects=True, vmem_limit_bytes=24 * 2**20
+            collective_id=1, has_side_effects=True, vmem_limit_bytes=6 * 2**20
         ),
         name="output",
     )(heads, weight)

time: 102 us -> 94.7 us (0.928); the launches traced: 100 us -> 95.1 us
  Pallas kernels: 91.5 us -> 84.6 us
  local copies, waits for them, and re-layouts: 8.57 us -> 10.1 us
    pallas_call x1, Pallas kernels: 25.6 us -> 12.5 us  [attend(): pl.pallas_call(functools.partial(attend_kernel, kv), out_shape=jax.ShapeD...]
    pallas_call x1, Pallas kernels: 44.5 us -> 50.1 us  [project(): pl.pallas_call(functools.partial(project_kernel, gx, yz, chunks), out_sha...]
    unnamed x12 -> x20, local copies, waits for them, and re-layouts: 7.87 us -> 9.42 us
where the time goes in v2:
time: 94.7 us; the launch traced here: 95.1 us
  Pallas kernels  84.6 us (89%)
  local copies, waits for them, and re-layouts  10.1 us (11%)
    pallas_call x1, Pallas kernels, project(): pl.pallas_call(functools.partial(project_kernel, gx, yz, chunks), out_sha...  50.1 us
    pallas_call x1, Pallas kernels, output(): pl.pallas_call(functools.partial(output_kernel, gx, yz, chunks), out_shap...  22.1 us
    pallas_call x1, Pallas kernels, attend(): pl.pallas_call(functools.partial(attend_kernel, kv), out_shape=jax.ShapeD...  12.5 us
    unnamed x20, local copies, waits for them, and re-layouts  9.42 us

profile of v2, /device:TPU:0, one launch (start us, length us, event | category | flops | bytes accessed | tf_op | source)
XLA Modules:
  0.0 95.1 jit_solution(2685029407329512876)
XLA Ops:
  0.0 0.7 reshape.17.gain_ref
  0.7 0.0 copy-start
  0.7 0.0 slice-start
  0.7 0.0 slice-start.1
  0.7 0.0 slice-start.2
  0.7 8.7 %copy.10 = bf16[1536,2,1792]{2,0,1:T(8,128)(2,1)S(1)} copy(bf16[1536,2,1792]{2,1,0:T(2,128)(2,1)} %param.9) | data formatting | bytes 22020096 | tf_op args[2]
  9.5 0.0 copy-start.1
  9.5 0.0 copy-done
  9.5 0.0 slice-start.3
  9.5 0.0 slice-start.4
  9.5 50.1 %project.1.proj_ref = f32[16,3584]{1,0:T(8,128)S(1)} custom-call(bf16[32,1536]{1,0:T(8,128)(2,1)S(1)} %copy-done, f32[1,1536]{1,0:T(1,128)S(1)} %reshape.17.gain_ref, bf16[2,1536,1792]{2,1,0:T(8,128)(2,1)S(1)} %bitcast.5), custom_call_target="tpu_custom_call" | custom-call | tf_op jit(solution)/shard_map/project/pallas_call | solution.py:160
  59.6 0.0 copy-done.1
  59.6 0.1 fusion
  59.7 0.1 pad_maximum_fusion
  59.8 0.0 slice-done
  59.8 0.0 slice-done.1
  59.8 0.0 slice-done.2
  59.8 0.0 slice-done.3
  59.8 0.0 slice-start.5
  59.9 0.0 slice-start.6
  59.9 12.5 %attend.1.heads_ref = bf16[16,3072]{1,0:T(8,128)(2,1)S(1)} custom-call(s32[16]{0:T(128)S(1)} %copy-done.1, f32[16,3584]{1,0:T(8,128)S(1)} %project.1.proj_ref, f32[16,128]{1,0:T(8,128)S(1)} %get-tuple-element.8.cos_ref, f32[16,128]{1,0:T(8,128)S(1)} %get-tuple-element.9.sin_ref, bf16[16,4096,128]{2,1,0:T(8,128)(2,1)S(1)} %bitcast.8, ...), custom_call_target="tpu_custom_call" | custom-call | tf_op jit(solution)/shard_map/attend/pallas_call | solution.py:302
  72.3 0.0 slice-done.4
  72.3 0.0 slice-done.5
  72.4 0.0 slice-done.6
  72.4 22.1 %output.1 = bf16[32,1536]{1,0:T(8,128)(2,1)S(1)} custom-call(bf16[16,3072]{1,0:T(8,128)(2,1)S(1)} %attend.1.heads_ref, bf16[3072,1536]{1,0:T(8,128)(2,1)S(1)} %bitcast.10), custom_call_target="tpu_custom_call" | custom-call | tf_op jit(solution)/shard_map/output/pallas_call | solution.py:406
  94.5 0.6 copy.12
  (4 shorter events, 0.0 us)
Async XLA Ops:
  0.7 8.8 %copy-start = (bf16[32,1536]{1,0:T(8,128)(2,1)S(1)}, bf16[32,1536]{1,0:T(8,128)(2,1)}, u32[]{:S(2)}) copy-start(bf16[32,1536]{1,0:T(8,128)(2,1)} %hidden_ref.1) | copy-start | bytes 294916
  0.7 59.1 %slice-start = ((s8[16777216]{0:T(1024)(128)(4,1)}), s8[4194304]{0:T(1024)(128)(4,1)S(1)}, s32[]{:S(2)}) async-start(s8[16777216]{0:T(1024)(128)(4,1)} %bitcast.6), calls=%async_computation | async-start | bytes 8388608
  0.7 59.1 %slice-start.1 = ((s8[16777216]{0:T(1024)(128)(4,1)}), s8[4194304]{0:T(1024)(128)(4,1)S(1)}, s32[]{:S(2)}) async-start(s8[16777216]{0:T(1024)(128)(4,1)} %bitcast.6), calls=%async_computation.1 | async-start | bytes 8388608
  0.7 59.1 %slice-start.2 = ((s8[16777216]{0:T(1024)(128)(4,1)}), s8[4194304]{0:T(1024)(128)(4,1)S(1)}, s32[]{:S(2)}) async-start(s8[16777216]{0:T(1024)(128)(4,1)} %bitcast.6), calls=%async_computation.2 | async-start | bytes 8388608
  9.5 50.1 %copy-start.1 = (s32[16]{0:T(128)S(1)}, s32[16]{0:T(128)}, u32[]{:S(2)}) copy-start(s32[16]{0:T(128)} %lengths_ref.1) | copy-start | bytes 196
  9.5 50.3 %slice-start.3 = ((s8[16777216]{0:T(1024)(128)(4,1)}), s8[4194304]{0:T(1024)(128)(4,1)S(1)}, s32[]{:S(2)}) async-start(s8[16777216]{0:T(1024)(128)(4,1)} %bitcast.6), calls=%async_computation.3 | async-start | bytes 8388608
  9.5 62.8 %slice-start.4 = ((s8[9437184]{0:T(1024)(128)(4,1)}), s8[1048576]{0:T(1024)(128)(4,1)S(1)}, s32[]{:S(2)}) async-start(s8[9437184]{0:T(1024)(128)(4,1)} %bitcast.9), calls=%async_computation.4 | async-start | bytes 2097152
  59.8 12.5 %slice-start.5 = ((s8[9437184]{0:T(1024)(128)(4,1)}), s8[4194304]{0:T(1024)(128)(4,1)S(1)}, s32[]{:S(2)}) async-start(s8[9437184]{0:T(1024)(128)(4,1)} %bitcast.9), calls=%async_computation.5 | async-start | bytes 8388608
  59.9 12.5 %slice-start.6 = ((s8[9437184]{0:T(1024)(128)(4,1)}), s8[4194304]{0:T(1024)(128)(4,1)S(1)}, s32[]{:S(2)}) async-start(s8[9437184]{0:T(1024)(128)(4,1)} %bitcast.9), calls=%async_computation.6 | async-start | bytes 8388608

commit v3 on v2

--- a/solution.py
+++ b/solution.py
@@ -152,7 +152,7 @@
     rows_each, depth = hidden.shape
     rows = rows_each * gx
     kv, _, columns = weight.shape
-    per = columns // 256
+    per = 2
     chunks = kv * per
     width = columns // per
     own = rows // yz

time: 94.7 us -> 88.5 us (0.935); the launches traced: 95.1 us -> 87.5 us
  Pallas kernels: 84.6 us -> 77 us
    pallas_call x1, Pallas kernels: 50.1 us -> 44.5 us  [project(): pl.pallas_call(functools.partial(project_kernel, gx, yz, chunks), out_sha...]
    pallas_call x1, Pallas kernels: 22.1 us -> 18.6 us  [output(): pl.pallas_call(functools.partial(output_kernel, gx, yz, chunks), out_shap...]
    pallas_call x1, Pallas kernels: 12.5 us -> 13.9 us  [attend(): pl.pallas_call(functools.partial(attend_kernel, kv), out_shape=jax.ShapeD...]
where the time goes in v3:
time: 88.5 us; the launch traced here: 87.5 us
  Pallas kernels  77 us (87%)
  local copies, waits for them, and re-layouts  10.1 us (11%)
    pallas_call x1, Pallas kernels, project(): pl.pallas_call(functools.partial(project_kernel, gx, yz, chunks), out_sha...  44.5 us
    pallas_call x1, Pallas kernels, output(): pl.pallas_call(functools.partial(output_kernel, gx, yz, chunks), out_shap...  18.6 us
    pallas_call x1, Pallas kernels, attend(): pl.pallas_call(functools.partial(attend_kernel, kv), out_shape=jax.ShapeD...  13.9 us
    unnamed x20, local copies, waits for them, and re-layouts  9.42 us

profile of v3, /device:TPU:0, one launch (start us, length us, event | category | flops | bytes accessed | tf_op | source)
XLA Modules:
  0.0 87.5 jit_solution(9155662127938730928)
XLA Ops:
  0.0 0.7 reshape.17.gain_ref
  0.7 0.0 copy-start
  0.7 0.0 slice-start
  0.7 0.0 slice-start.1
  0.7 0.0 slice-start.2
  0.7 8.7 %copy.10 = bf16[1536,2,1792]{2,0,1:T(8,128)(2,1)S(1)} copy(bf16[1536,2,1792]{2,1,0:T(2,128)(2,1)} %param.9) | data formatting | bytes 22020096 | tf_op args[2]
  9.5 0.0 copy-start.1
  9.5 0.0 copy-done
  9.5 0.0 slice-start.3
  9.5 0.0 slice-start.4
  9.5 44.5 %project.1.proj_ref = f32[16,3584]{1,0:T(8,128)S(1)} custom-call(bf16[32,1536]{1,0:T(8,128)(2,1)S(1)} %copy-done, f32[1,1536]{1,0:T(1,128)S(1)} %reshape.17.gain_ref, bf16[2,1536,1792]{2,1,0:T(8,128)(2,1)S(1)} %bitcast.5), custom_call_target="tpu_custom_call" | custom-call | tf_op jit(solution)/shard_map/project/pallas_call | solution.py:160
  54.0 0.0 copy-done.1
  54.0 0.1 fusion
  54.1 0.1 pad_maximum_fusion
  54.2 0.0 slice-done
  54.2 0.0 slice-done.1
  54.2 0.0 slice-done.2
  54.2 0.0 slice-done.3
  54.2 0.0 slice-start.5
  54.3 0.0 slice-start.6
  54.3 13.9 %attend.1.heads_ref = bf16[16,3072]{1,0:T(8,128)(2,1)S(1)} custom-call(s32[16]{0:T(128)S(1)} %copy-done.1, f32[16,3584]{1,0:T(8,128)S(1)} %project.1.proj_ref, f32[16,128]{1,0:T(8,128)S(1)} %get-tuple-element.8.cos_ref, f32[16,128]{1,0:T(8,128)S(1)} %get-tuple-element.9.sin_ref, bf16[16,4096,128]{2,1,0:T(8,128)(2,1)S(1)} %bitcast.8, ...), custom_call_target="tpu_custom_call" | custom-call | tf_op jit(solution)/shard_map/attend/pallas_call | solution.py:302
  68.2 0.0 slice-done.4
  68.2 0.0 slice-done.5
  68.2 0.0 slice-done.6
  68.2 18.6 %output.1 = bf16[32,1536]{1,0:T(8,128)(2,1)S(1)} custom-call(bf16[16,3072]{1,0:T(8,128)(2,1)S(1)} %attend.1.heads_ref, bf16[3072,1536]{1,0:T(8,128)(2,1)S(1)} %bitcast.10), custom_call_target="tpu_custom_call" | custom-call | tf_op jit(solution)/shard_map/output/pallas_call | solution.py:406
  86.9 0.6 copy.12
  (4 shorter events, 0.0 us)
Async XLA Ops:
  0.7 8.8 %copy-start = (bf16[32,1536]{1,0:T(8,128)(2,1)S(1)}, bf16[32,1536]{1,0:T(8,128)(2,1)}, u32[]{:S(2)}) copy-start(bf16[32,1536]{1,0:T(8,128)(2,1)} %hidden_ref.1) | copy-start | bytes 294916
  0.7 53.5 %slice-start = ((s8[16777216]{0:T(1024)(128)(4,1)}), s8[4194304]{0:T(1024)(128)(4,1)S(1)}, s32[]{:S(2)}) async-start(s8[16777216]{0:T(1024)(128)(4,1)} %bitcast.6), calls=%async_computation | async-start | bytes 8388608
  0.7 53.5 %slice-start.1 = ((s8[16777216]{0:T(1024)(128)(4,1)}), s8[4194304]{0:T(1024)(128)(4,1)S(1)}, s32[]{:S(2)}) async-start(s8[16777216]{0:T(1024)(128)(4,1)} %bitcast.6), calls=%async_computation.1 | async-start | bytes 8388608
  0.7 53.5 %slice-start.2 = ((s8[16777216]{0:T(1024)(128)(4,1)}), s8[4194304]{0:T(1024)(128)(4,1)S(1)}, s32[]{:S(2)}) async-start(s8[16777216]{0:T(1024)(128)(4,1)} %bitcast.6), calls=%async_computation.2 | async-start | bytes 8388608
  9.5 44.5 %copy-start.1 = (s32[16]{0:T(128)S(1)}, s32[16]{0:T(128)}, u32[]{:S(2)}) copy-start(s32[16]{0:T(128)} %lengths_ref.1) | copy-start | bytes 196
  9.5 44.7 %slice-start.3 = ((s8[16777216]{0:T(1024)(128)(4,1)}), s8[4194304]{0:T(1024)(128)(4,1)S(1)}, s32[]{:S(2)}) async-start(s8[16777216]{0:T(1024)(128)(4,1)} %bitcast.6), calls=%async_computation.3 | async-start | bytes 8388608
  9.5 58.7 %slice-start.4 = ((s8[9437184]{0:T(1024)(128)(4,1)}), s8[1048576]{0:T(1024)(128)(4,1)S(1)}, s32[]{:S(2)}) async-start(s8[9437184]{0:T(1024)(128)(4,1)} %bitcast.9), calls=%async_computation.4 | async-start | bytes 2097152
  54.2 14.0 %slice-start.5 = ((s8[9437184]{0:T(1024)(128)(4,1)}), s8[4194304]{0:T(1024)(128)(4,1)S(1)}, s32[]{:S(2)}) async-start(s8[9437184]{0:T(1024)(128)(4,1)} %bitcast.9), calls=%async_computation.5 | async-start | bytes 8388608
  54.3 14.0 %slice-start.6 = ((s8[9437184]{0:T(1024)(128)(4,1)}), s8[4194304]{0:T(1024)(128)(4,1)S(1)}, s32[]{:S(2)}) async-start(s8[9437184]{0:T(1024)(128)(4,1)} %bitcast.9), calls=%async_computation.6 | async-start | bytes 8388608

commit v4 on v3

--- a/solution.py
+++ b/solution.py
@@ -183,7 +183,7 @@
     )(hidden, gain, weight)
 
 
-CHUNK = 512
+CHUNK = 256
 
 
 def attend_kernel(

time: 88.5 us -> 89.5 us (1.011); the launches traced: 87.5 us -> 89.9 us
  Pallas kernels: 77 us -> 79.4 us
    pallas_call x1, Pallas kernels: 18.6 us -> 21.9 us  [output(): pl.pallas_call(functools.partial(output_kernel, gx, yz, chunks), out_shap...]
where the time goes in v4:
time: 89.5 us; the launch traced here: 89.9 us
  Pallas kernels  79.4 us (89%)
  local copies, waits for them, and re-layouts  10.1 us (11%)
    pallas_call x1, Pallas kernels, project(): pl.pallas_call(functools.partial(project_kernel, gx, yz, chunks), out_sha...  44.5 us
    pallas_call x1, Pallas kernels, output(): pl.pallas_call(functools.partial(output_kernel, gx, yz, chunks), out_shap...  21.9 us
    pallas_call x1, Pallas kernels, attend(): pl.pallas_call(functools.partial(attend_kernel, kv), out_shape=jax.ShapeD...  13.1 us
    unnamed x20, local copies, waits for them, and re-layouts  9.42 us

profile of v4, /device:TPU:0, one launch (start us, length us, event | category | flops | bytes accessed | tf_op | source)
XLA Modules:
  0.0 89.9 jit_solution(2133799302124588981)
XLA Ops:
  0.0 0.7 reshape.17.gain_ref
  0.7 0.0 copy-start
  0.7 0.0 slice-start
  0.7 0.0 slice-start.1
  0.7 0.0 slice-start.2
  0.7 8.7 %copy.10 = bf16[1536,2,1792]{2,0,1:T(8,128)(2,1)S(1)} copy(bf16[1536,2,1792]{2,1,0:T(2,128)(2,1)} %param.9) | data formatting | bytes 22020096 | tf_op args[2]
  9.5 0.0 copy-start.1
  9.5 0.0 copy-done
  9.5 0.0 slice-start.3
  9.5 0.0 slice-start.4
  9.5 44.5 %project.1.proj_ref = f32[16,3584]{1,0:T(8,128)S(1)} custom-call(bf16[32,1536]{1,0:T(8,128)(2,1)S(1)} %copy-done, f32[1,1536]{1,0:T(1,128)S(1)} %reshape.17.gain_ref, bf16[2,1536,1792]{2,1,0:T(8,128)(2,1)S(1)} %bitcast.5), custom_call_target="tpu_custom_call" | custom-call | tf_op jit(solution)/shard_map/project/pallas_call | solution.py:160
  54.0 0.0 copy-done.1
  54.0 0.1 fusion
  54.1 0.1 pad_maximum_fusion
  54.2 0.0 slice-done
  54.2 0.0 slice-done.1
  54.2 0.0 slice-done.2
  54.2 0.0 slice-done.3
  54.2 0.0 slice-start.5
  54.3 0.0 slice-start.6
  54.3 13.1 %attend.1.heads_ref = bf16[16,3072]{1,0:T(8,128)(2,1)S(1)} custom-call(s32[16]{0:T(128)S(1)} %copy-done.1, f32[16,3584]{1,0:T(8,128)S(1)} %project.1.proj_ref, f32[16,128]{1,0:T(8,128)S(1)} %get-tuple-element.8.cos_ref, f32[16,128]{1,0:T(8,128)S(1)} %get-tuple-element.9.sin_ref, bf16[16,4096,128]{2,1,0:T(8,128)(2,1)S(1)} %bitcast.8, ...), custom_call_target="tpu_custom_call" | custom-call | tf_op jit(solution)/shard_map/attend/pallas_call | solution.py:302
  67.4 0.0 slice-done.4
  67.4 0.0 slice-done.5
  67.4 0.0 slice-done.6
  67.4 21.9 %output.1 = bf16[32,1536]{1,0:T(8,128)(2,1)S(1)} custom-call(bf16[16,3072]{1,0:T(8,128)(2,1)S(1)} %attend.1.heads_ref, bf16[3072,1536]{1,0:T(8,128)(2,1)S(1)} %bitcast.10), custom_call_target="tpu_custom_call" | custom-call | tf_op jit(solution)/shard_map/output/pallas_call | solution.py:406
  89.3 0.6 copy.12
  (4 shorter events, 0.0 us)
Async XLA Ops:
  0.7 8.8 %copy-start = (bf16[32,1536]{1,0:T(8,128)(2,1)S(1)}, bf16[32,1536]{1,0:T(8,128)(2,1)}, u32[]{:S(2)}) copy-start(bf16[32,1536]{1,0:T(8,128)(2,1)} %hidden_ref.1) | copy-start | bytes 294916
  0.7 53.5 %slice-start = ((s8[16777216]{0:T(1024)(128)(4,1)}), s8[4194304]{0:T(1024)(128)(4,1)S(1)}, s32[]{:S(2)}) async-start(s8[16777216]{0:T(1024)(128)(4,1)} %bitcast.6), calls=%async_computation | async-start | bytes 8388608
  0.7 53.5 %slice-start.1 = ((s8[16777216]{0:T(1024)(128)(4,1)}), s8[4194304]{0:T(1024)(128)(4,1)S(1)}, s32[]{:S(2)}) async-start(s8[16777216]{0:T(1024)(128)(4,1)} %bitcast.6), calls=%async_computation.1 | async-start | bytes 8388608
  0.7 53.5 %slice-start.2 = ((s8[16777216]{0:T(1024)(128)(4,1)}), s8[4194304]{0:T(1024)(128)(4,1)S(1)}, s32[]{:S(2)}) async-start(s8[16777216]{0:T(1024)(128)(4,1)} %bitcast.6), calls=%async_computation.2 | async-start | bytes 8388608
  9.5 44.5 %copy-start.1 = (s32[16]{0:T(128)S(1)}, s32[16]{0:T(128)}, u32[]{:S(2)}) copy-start(s32[16]{0:T(128)} %lengths_ref.1) | copy-start | bytes 196
  9.5 44.7 %slice-start.3 = ((s8[16777216]{0:T(1024)(128)(4,1)}), s8[4194304]{0:T(1024)(128)(4,1)S(1)}, s32[]{:S(2)}) async-start(s8[16777216]{0:T(1024)(128)(4,1)} %bitcast.6), calls=%async_computation.3 | async-start | bytes 8388608
  9.5 57.9 %slice-start.4 = ((s8[9437184]{0:T(1024)(128)(4,1)}), s8[1048576]{0:T(1024)(128)(4,1)S(1)}, s32[]{:S(2)}) async-start(s8[9437184]{0:T(1024)(128)(4,1)} %bitcast.9), calls=%async_computation.4 | async-start | bytes 2097152
  54.2 13.1 %slice-start.5 = ((s8[9437184]{0:T(1024)(128)(4,1)}), s8[4194304]{0:T(1024)(128)(4,1)S(1)}, s32[]{:S(2)}) async-start(s8[9437184]{0:T(1024)(128)(4,1)} %bitcast.9), calls=%async_computation.5 | async-start | bytes 8388608
  54.3 13.1 %slice-start.6 = ((s8[9437184]{0:T(1024)(128)(4,1)}), s8[4194304]{0:T(1024)(128)(4,1)S(1)}, s32[]{:S(2)}) async-start(s8[9437184]{0:T(1024)(128)(4,1)} %bitcast.9), calls=%async_computation.6 | async-start | bytes 8388608
